TPU v7x, 32 devices: a whole 2x2x4 slice. The times are simulated.
32 devices in a mesh: wave: 4 (over y, x), strip: 8 (over z, core).
Axes of the slice: x: 2, y: 2, z: 4, core: 2. Of those that a mesh axis runs over, the one named last changes fastest.
Arguments:
- unit_params: float32 [9, 8, 24576], P(None, 'strip', 'wave'), may hold values from 0 to 1
- observed: bfloat16 [4, 256, 768, 256], P(None, 'wave', 'strip'), may hold values from -3 to 3
- psf_rows: bfloat16 [256, 4, 65], P('wave'), may hold values from -0.75 to 0.75
- psf_cols: bfloat16 [256, 4, 65], P('wave'), may hold values from -0.75 to 0.75
- pixel_mask: int32 [768, 256], P('strip'), may hold values 0 or 1
- strip_lengths: int32 [8], P('strip'), may hold values from 32 to 96, as said below
Outputs:
- param_grad: float32 [9, 8, 24576], P(None, 'strip', 'wave')
Inputs may be any that keep to these rules, and one draw needn't show every extreme that they name: `strip_lengths`: the strip lengths sum to 512; in every draw one strip holds 96 rows and one holds 32.
All inputs are finite; a program needn't handle non-finite values. No bound on the sum of `pixel_mask` on one device may be relied on, other than what follows from the above.
Results may differ from a plain program's by a relative error of at most 0.00098.
Values may be sent and summed in bfloat16 or wider, within the bound.
A program may use at most 192 MiB of HBM per device.

v0:
```python
import jax
import jax.numpy as jnp
from jax import lax
from jax.sharding import PartitionSpec as P

parameter_low = (0.2, 0.4, 2.0, -0.8, 0.4, 0.3, 0.0, 0.0, 0.0)
parameter_span = (0.4, 0.6, 18.0, 1.6, 0.8, 1.2, 1.5, 3.141592653589793, 3.141592653589793)
stokes_weight = (1.0, 3.0, 3.0, 2.0)
loss_scale = 0.03125


def passed_along(shard, axis, by):
    count = lax.axis_size(axis)
    pairs = [(i, i + by) for i in range(count) if 0 <= i + by < count]
    return lax.ppermute(shard, axis, pairs)


def profile(distance, damping):
    scaled = distance / damping
    return 1.0 / (1.0 + scaled * scaled)


def stokes_model(unit_params, wave_grid):
    physical = [
        parameter_low[number] + parameter_span[number] * unit_params[number] for number in range(9)
    ]
    (
        source_zero,
        source_slope,
        strength,
        doppler,
        line_width,
        damping,
        zeeman_split,
        incline,
        azimuth,
    ) = physical
    offset = (wave_grid[:, None, None] - doppler) / line_width
    split_ratio = zeeman_split / line_width
    centre = profile(offset, damping)
    upper_line = profile(offset - split_ratio, damping)
    lower_line = profile(offset + split_ratio, damping)
    cosine = jnp.cos(incline)
    sine_value = jnp.sin(incline)
    sine_square = sine_value * sine_value
    absorb_total = 1.0 + strength * (
        centre * sine_square * 0.5 + (upper_line + lower_line) * (1.0 + cosine * cosine) * 0.25
    )
    linear = strength * (centre - 0.5 * (upper_line + lower_line)) * sine_square * 0.5
    linear_cosine = linear * jnp.cos(2.0 * azimuth)
    linear_sine = linear * jnp.sin(2.0 * azimuth)
    circular = strength * (lower_line - upper_line) * cosine * 0.5
    denominator = (
        absorb_total * absorb_total
        - linear_cosine * linear_cosine
        - linear_sine * linear_sine
        - circular * circular
    )
    source_ratio = source_slope / denominator
    return jnp.stack(
        [
            source_zero + source_ratio * absorb_total,
            -source_ratio * linear_cosine,
            -source_ratio * linear_sine,
            -source_ratio * circular,
        ]
    )


def band_tables(tap_table, out_rows, tap_count):
    in_rows = out_rows + tap_count - 1
    target_row = lax.broadcasted_iota(jnp.int32, (out_rows, in_rows, tap_count), 0)
    source_row = lax.broadcasted_iota(jnp.int32, (out_rows, in_rows, tap_count), 1)
    tap_index = lax.broadcasted_iota(jnp.int32, (out_rows, in_rows, tap_count), 2)
    selector = (source_row - target_row == tap_index).astype(jnp.bfloat16)
    return jnp.einsum(
        "wkt,ijt->wkij", tap_table, selector, preferred_element_type=jnp.float32
    ).astype(jnp.bfloat16)


def column_tables(tap_table, columns, tap_count):
    radius = tap_count // 2
    source_column = lax.broadcasted_iota(jnp.int32, (columns, columns, tap_count), 0)
    target_column = lax.broadcasted_iota(jnp.int32, (columns, columns, tap_count), 1)
    tap_index = lax.broadcasted_iota(jnp.int32, (columns, columns, tap_count), 2)
    selector = (source_column - target_column + radius == tap_index).astype(jnp.bfloat16)
    return jnp.einsum(
        "wkt,xyt->wkxy", tap_table, selector, preferred_element_type=jnp.float32
    ).astype(jnp.bfloat16)


def extend(upper_rim, middle, lower_rim, length, axis_index):
    radius = upper_rim.shape[axis_index]
    widened = jnp.concatenate([upper_rim, middle, jnp.zeros_like(upper_rim)], axis=axis_index)
    return lax.dynamic_update_slice_in_dim(widened, lower_rim, radius + length, axis_index)


def per_device(unit_params, observed, psf_rows, psf_cols, pixel_mask, strip_lengths):
    stokes_count, wave_count, capacity, columns = observed.shape
    tap_count = psf_rows.shape[2]
    radius = tap_count // 2
    gathered = lax.all_gather(unit_params, "wave", axis=2, tiled=True)
    own_params = gathered.reshape(gathered.shape[0], capacity, columns)
    length = strip_lengths[0]
    strip_pos = lax.axis_index("strip")
    strip_total = lax.axis_size("strip")
    wave_pos = lax.axis_index("wave")
    levels = (wave_pos * wave_count + jnp.arange(wave_count, dtype=jnp.int32)).astype(jnp.float32)
    wave_grid = -3.0 + 6.0 * levels / (wave_count * lax.axis_size("wave") - 1)
    row_index = jnp.arange(capacity, dtype=jnp.int32)
    rows_live = (row_index < length).astype(jnp.float32)
    wide_index = jnp.arange(capacity + 2 * radius, dtype=jnp.int32)
    live_wide = (
        (wide_index < radius) & (strip_pos > 0)
        | (wide_index >= radius) & (wide_index < radius + length)
        | (wide_index >= radius + length)
        & (wide_index < 2 * radius + length)
        & (strip_pos < strip_total - 1)
    )
    live_float = live_wide.astype(jnp.float32)
    tail_rows = lax.dynamic_slice_in_dim(own_params, length - radius, radius, 1)
    upper_rim = passed_along(tail_rows, "strip", 1)
    lower_rim = passed_along(own_params[:, :radius], "strip", -1)
    params_wide = extend(upper_rim, own_params, lower_rim, length, 1)
    model_wide = (stokes_model(params_wide, wave_grid) * live_float[:, None]).astype(jnp.bfloat16)
    row_band = band_tables(psf_rows, capacity, tap_count)
    column_band = column_tables(psf_cols, columns, tap_count)
    live_mask = pixel_mask.astype(jnp.float32) * rows_live[:, None]
    weight_square = jnp.array(stokes_weight, jnp.float32)
    weight_square = weight_square * weight_square
    block_size = 4
    block_count = wave_count // block_size

    def forward(number, residual_all):
        first_wave = number * block_size
        model_block = lax.dynamic_slice_in_dim(model_wide, first_wave, block_size, 1)
        band_block = lax.dynamic_slice_in_dim(row_band, first_wave, block_size, 0)
        column_block = lax.dynamic_slice_in_dim(column_band, first_wave, block_size, 0)
        observed_block = lax.dynamic_slice_in_dim(observed, first_wave, block_size, 1)
        row_pass = jnp.einsum(
            "wkij,swjc->kswic", band_block, model_block, preferred_element_type=jnp.float32
        ).astype(jnp.bfloat16)
        blurred = jnp.einsum(
            "kswic,wkcd->swid", row_pass, column_block, preferred_element_type=jnp.float32
        )
        residual = (
            loss_scale
            * weight_square[:, None, None, None]
            * live_mask
            * (blurred - observed_block.astype(jnp.float32))
        ).astype(jnp.bfloat16)
        return lax.dynamic_update_slice_in_dim(residual_all, residual, first_wave, 1)

    residual_all = lax.fori_loop(0, block_count, forward, jnp.zeros(observed.shape, jnp.bfloat16))
    row_back = band_tables(psf_rows[:, :, ::-1], capacity, tap_count)
    tail_residual = lax.dynamic_slice_in_dim(residual_all, length - radius, radius, 2)
    upper_resid = passed_along(tail_residual, "strip", 1)
    lower_resid = passed_along(residual_all[:, :, :radius], "strip", -1)
    residual_wide = extend(upper_resid, residual_all, lower_resid, length, 2)

    def backward(number, gradient_sum):
        first_wave = number * block_size
        residual_block = lax.dynamic_slice_in_dim(residual_wide, first_wave, block_size, 1)
        column_block = lax.dynamic_slice_in_dim(column_band, first_wave, block_size, 0)
        back_block = lax.dynamic_slice_in_dim(row_back, first_wave, block_size, 0)
        grid_block = lax.dynamic_slice_in_dim(wave_grid, first_wave, block_size, 0)
        across = jnp.einsum(
            "swjc,wkdc->kswjd", residual_block, column_block, preferred_element_type=jnp.float32
        ).astype(jnp.bfloat16)
        adjoint = (
            jnp.einsum("wkij,kswjc->swic", back_block, across, preferred_element_type=jnp.float32)
            * rows_live[:, None]
        )

        def model_of(params_now):
            return stokes_model(params_now, grid_block)

        unused_model, pullback = jax.vjp(model_of, own_params)
        return gradient_sum + pullback(adjoint)[0]

    gradient_local = lax.fori_loop(
        0, block_count, backward, jnp.zeros(own_params.shape, jnp.float32)
    )
    gradient_flat = gradient_local.reshape(gathered.shape)
    gradient_total = lax.psum(gradient_flat, "wave")
    share_width = unit_params.shape[2]
    return lax.dynamic_slice_in_dim(gradient_total, wave_pos * share_width, share_width, 2)


def solution(mesh):
    return jax.shard_map(
        per_device,
        mesh=mesh,
        in_specs=(
            P(None, "strip", "wave"),
            P(None, "wave", "strip", None),
            P("wave", None, None),
            P("wave", None, None),
            P("strip", None),
            P("strip"),
        ),
        out_specs=P(None, "strip", "wave"),
        check_vma=False,
    )
```

profile of v0, /device:TPU:17, one launch (start us, length us, event | category | flops | bytes accessed | tf_op | source)
XLA Modules:
  0.0 684.5 jit_solution(11187282469692166025)
XLA Ops:
  7.2 12.0 %all_gather.3 = f32[9,1,24576]{2,1,0:T(1,128)S(1)} all-gather(f32[9,1,6144]{2,1,0:T(1,128)} %param.11), channel_id=1, replica_groups=mesh['wave'=4,'strip'=8] {'wave'}, dimensions={2}, use_global_device_ids=true | all-gather | bytes 1105920 | tf_op jit(solution)/shard_map/all_gather | solution.py:102
  23.1 4.9 collective-permute-start
  31.2 15.3 %convert_bitcast_fusion = bf16[64,4,256,256]{3,0,1,2:T(8,128)(2,1)} fusion(bf16[64,4,65]{2,1,0:T(4,128)(2,1)} %param.14), kind=kOutput, calls=%fused_computation.148 | convolution fusion | flops 2210594816 | bytes 33587712 | tf_op jit(solution)/shard_map/wkt,xyt->wkxy/dot_general | solution.py:87
  46.5 5.5 convert_bitcast_fusion.2
  52.1 23.0 %copy.20 = bf16[64,4,256,256]{3,2,1,0:T(8,128)(2,1)} copy(bf16[64,4,256,256]{3,0,1,2:T(8,128)(2,1)} %convert_bitcast_fusion) | data formatting | bytes 67108864
  75.3 3.2 dynamic_update_slice.13
  79.9 18.9 %multiply_add_fusion.8 = (f32[1,64,160,256]{3,2,1,0:T(8,128)S(1)}, f32[1,64,160,256]{3,2,1,0:T(8,128)S(1)}, f32[1,64,160,256]{3,2,1,0:T(8,128)S(1)}, f32[1,64,160,256]{3,2,1,0:T(8,128)}) fusion(f32[160,256]{1,0:T(8,128)S(1)} %get-tuple-element.534, f32[160,256]{1,0:T(8,128)S(1)} %get-tuple-element.538, f32[160,256]{1,0:T(8,128)S(1)} %get-tuple-element.536, ...), kind=kLoop, calls=%fused_computation.159 | loop fusion | flops 125829120 | bytes 44073216 | tf_op jit(solution)/shard_map/add | solution.py:62
  98.8 15.2 %fusion.71 = bf16[4,64,160,256]{3,2,1,0:T(8,128)(2,1)} fusion(f32[1,64,160,256]{3,2,1,0:T(8,128)S(1)} %get-tuple-element.528, f32[1,64,160,256]{3,2,1,0:T(8,128)S(1)} %get-tuple-element.529, f32[1,64,160,256]{3,2,1,0:T(8,128)} %get-tuple-element.530, f32[1,64,160,256]{3,2,1,0:T(8,128)S(1)} %get-tuple-element.527, f32[160]{0:T(256)S(1)} %or_convert_fusion), kind=kLoop, calls=%fused_computation.147 | loop fusion | flops 52428800 | bytes 62915200 | tf_op jit(solution)/shard_map/convert_element_type | solution.py:125
  114.0 6.0 broadcast_in_dim.111.clone
  120.0 116.9 %while.31 = (s32[]{:T(128)}, bf16[4,64,96,256]{3,2,1,0:T(8,128)(2,1)}, f32[96,256]{1,0:T(8,128)S(1)}, bf16[64,4,256,256]{3,2,1,0:T(8,128)(2,1)}, bf16[4,64,160,2...) while((s32[]{:T(128)}, ...), condition=%wide.region_1.0_spmd.clone, body=%wide.region_0.0_spmd.clone.sunk | while | flops 1311866880 | bytes 9897691 | solution.py:154
  122.4 4.0 fusion.123
  129.8 4.0 fusion.123
  137.1 4.0 fusion.123
  144.3 4.0 fusion.123
  151.7 4.0 fusion.123
  159.0 4.0 fusion.123
  166.3 4.0 fusion.123
  173.6 4.0 fusion.123
  180.9 4.0 fusion.123
  188.2 3.9 fusion.123
  195.5 4.0 fusion.123
  202.8 4.0 fusion.123
  210.1 4.0 fusion.123
  217.4 4.0 fusion.123
  224.7 3.9 fusion.123
  232.0 4.0 fusion.123
  237.0 9.9 %fusion.107 = (bf16[4,64,32,256]{3,2,1,0:T(8,128)(2,1)}, bf16[4,64,32,256]{3,2,1,0:T(8,128)(2,1)}) fusion(bf16[4,64,96,256]{3,2,1,0:T(8,128)(2,1)} %get-tuple-element.364, s32[]{:T(128)S(6)} %select_n.36), kind=kLoop, calls=%fused_computation.218 | loop fusion | bytes 16777220 | tf_op jit(solution)/shard_map/slice | solution.py:158
  246.9 3.0 collective-permute-start.2
  252.1 5.5 convert_bitcast_fusion.1
  257.6 38.0 %collective-permute-done.2 = bf16[4,64,32,256]{3,2,1,0:T(8,128)(2,1)} collective-permute-done((bf16[4,64,32,256]{3,2,1,0:T(8,128)(2,1)}, bf16[4,64,32,256]{3,2,1,0:T(8,128)(2,1)}, u32[]{:S(2)}, u32[]{:S(2)}) %collective-permute-start.2) | collective-permute-done | bytes 4194336 | tf_op jit(solution)/shard_map/ppermute | solution.py:15
  295.6 18.3 %maximum_maximum_fusion = bf16[4,64,160,256]{3,2,1,0:T(8,128)(2,1)} fusion(bf16[4,64,96,256]{3,2,1,0:T(8,128)(2,1)} %get-tuple-element.364, bf16[4,64,32,256]{3,2,1,0:T(8,128)(2,1)} %collective-permute-done.2, bf16[160]{0:T(256)(128)(2,1)S(1)} %pad.110.clone), kind=kLoop, calls=%fused_computation.149 | loop fusion | flops 62914560 | bytes 37749056 | tf_op jit(solution)/shard_map/concatenate | solution.py:94
  314.0 40.0 %dynamic_update_slice.14 = bf16[4,64,160,256]{3,2,1,0:T(8,128)(2,1)} dynamic-update-slice(bf16[4,64,160,256]{3,2,1,0:T(8,128)(2,1)} %maximum_maximum_fusion, bf16[4,64,32,256]{3,2,1,0:T(8,128)(2,1)} %collective-permute-done.3, s32[]{:T(128)} %constant.284.clone.1, s32[]{:T(128)} %constant.284.clone.1, s32[]{:T(128)S(6)} %select_n.37, s32[]{:T(128)} %constant.284.clone.1) | dynamic-update-slice | bytes 8388612 | tf_op jit(solution)/shard_map/dynamic_update_slice | solution.py:95
  354.0 269.4 %while.32 = (s32[]{:T(128)}, f32[9,96,256]{2,1,0:T(8,128)S(1)}, f32[9,96,256]{2,1,0:T(8,128)S(1)}, f32[64]{0:T(128)S(1)}, bf16[64,4,256,256]{3,2,1,0:T(8,128)(2,...) while((s32[]{:T(128)}, f32[9,96,256]{2,1,0:T(8,128)S(1)}, ...), condition=%wide.region_21.22_spmd.clone, body=%wide.region_2.21_spmd.clone.sunk | while | flops 1872642304 | bytes 34342920 | solution.py:181
  357.2 4.9 fusion.127
  370.8 2.5 constant_dynamic-slice_fusion.12
  374.0 4.9 fusion.127
  387.7 2.5 constant_dynamic-slice_fusion.12
  390.9 4.9 fusion.127
  404.5 2.5 constant_dynamic-slice_fusion.12
  407.7 4.9 fusion.127
  421.4 2.5 constant_dynamic-slice_fusion.12
  424.5 4.9 fusion.127
  438.2 2.5 constant_dynamic-slice_fusion.12
  441.4 4.9 fusion.127
  455.0 2.5 constant_dynamic-slice_fusion.12
  458.2 4.9 fusion.127
  471.9 2.5 constant_dynamic-slice_fusion.12
  475.1 4.9 fusion.127
  488.7 2.5 constant_dynamic-slice_fusion.12
  491.9 4.9 fusion.127
  505.6 2.5 constant_dynamic-slice_fusion.12
  508.7 4.9 fusion.127
  522.4 2.5 constant_dynamic-slice_fusion.12
  525.6 4.9 fusion.127
  539.2 2.5 constant_dynamic-slice_fusion.12
  542.4 4.9 fusion.127
  556.1 2.5 constant_dynamic-slice_fusion.12
  559.3 4.9 fusion.127
  576.1 4.9 fusion.127
  589.8 2.5 constant_dynamic-slice_fusion.12
  592.9 4.9 fusion.127
  606.6 2.5 constant_dynamic-slice_fusion.12
  609.8 4.9 fusion.127
  625.3 50.7 %all-reduce.11.cloned.1.call-done = f32[9,1,24576]{2,1,0:T(1,128)} async-done(((f32[9,1,24576]{2,1,0:T(1,128)}), f32[9,1,24576]{2,1,0:T(1,128)}) %all-reduce.11.cloned.1.call-update) | async-done | bytes 884752 | tf_op jit(solution)/shard_map/psum | solution.py:185
  (343 shorter events, 222.2 us)
Async XLA Ops:
  6.5 669.5 %all-reduce.11.cloned.1.call-start = ((), (), s32[]{:S(2)}) async-start(), calls=%async_computation | async-start | bytes 1769472 | tf_op jit(solution)/shard_map/psum | solution.py:185
  21.8 1.2 copy-start
  23.1 52.0 %collective-permute-start = (f32[9,32,256]{2,1,0:T(8,128)S(1)}, f32[9,32,256]{2,1,0:T(8,128)S(1)}, u32[]{:S(2)}, u32[]{:S(2)}) collective-permute-start(f32[9,32,256]{2,1,0:T(8,128)S(1)} %constant_dynamic-slice_fusion.5), channel_id=1, source_target_pairs={{0,1},{1,2},{2,3},{3,4},{4,5},{5,6},{6,7},{8,9},{9,10},{10,11},{11... | collective-permute-start | bytes 884744 | tf_op jit(solution)/shard_map/ppermute | solution.py:15
  29.0 46.2 %collective-permute-start.1 = (f32[9,32,256]{2,1,0:T(8,128)S(1)}, f32[9,32,256]{2,1,0:T(8,128)S(1)}, u32[]{:S(2)}, u32[]{:S(2)}) collective-permute-start(f32[9,32,256]{2,1,0:T(8,128)S(1)} %slice.140), channel_id=1, source_target_pairs={{1,0},{2,1},{3,2},{4,3},{5,4},{6,5},{7,6},{9,8},{10,9},{11,10},{12... | collective-permute-start | bytes 884744 | tf_op jit(solution)/shard_map/ppermute | solution.py:15
  31.2 15.3 %copy-start.1 = (bf16[64,4,65]{2,1,0:T(4,128)(2,1)S(1)}, bf16[64,4,65]{2,1,0:T(4,128)(2,1)}, u32[]{:S(2)}) copy-start(bf16[64,4,65]{2,1,0:T(4,128)(2,1)} %param.13) | copy-start | bytes 99844
  46.5 5.5 copy-start.3
  114.0 6.0 copy-start.4
  237.0 14.9 %copy-start.2 = (bf16[64,4,65]{2,1,0:T(4,128)(2,1)S(1)}, bf16[64,4,65]{2,1,0:T(4,128)(2,1)}, u32[]{:S(2)}) copy-start(bf16[64,4,65]{2,1,0:T(4,128)(2,1)} %param.13) | copy-start | bytes 99844
  246.9 48.8 %collective-permute-start.2 = (bf16[4,64,32,256]{3,2,1,0:T(8,128)(2,1)}, bf16[4,64,32,256]{3,2,1,0:T(8,128)(2,1)}, u32[]{:S(2)}, u32[]{:S(2)}) collective-permute-start(bf16[4,64,32,256]{3,2,1,0:T(8,128)(2,1)} %get-tuple-element.526), channel_id=1, source_target_pairs={{0,1},{1,2},{2,3},{3,4},{4,5},{5,6},{6,7},{8,9},{9,10},{10,11},{11... | collective-permute-start | bytes 12582920 | tf_op jit(solution)/shard_map/ppermute | solution.py:15
  249.9 64.1 %collective-permute-start.3 = (bf16[4,64,32,256]{3,2,1,0:T(8,128)(2,1)}, bf16[4,64,32,256]{3,2,1,0:T(8,128)(2,1)}, u32[]{:S(2)}, u32[]{:S(2)}) collective-permute-start(bf16[4,64,32,256]{3,2,1,0:T(8,128)(2,1)} %get-tuple-element.525), channel_id=1, source_target_pairs={{1,0},{2,1},{3,2},{4,3},{5,4},{6,5},{7,6},{9,8},{10,9},{11,10},{12... | collective-permute-start | bytes 12582920 | tf_op jit(solution)/shard_map/ppermute | solution.py:15
Sparse Core Ops, SparseCore 0:
  625.4 50.5 all-reduce.10
where the time goes:
time: 691 us; the launch traced here: 685 us
  other arithmetic  206 us (30%)
  local copies, waits for them, and re-layouts  182 us (26%)
  matrix products  168 us (24%)
  waiting for transfers between devices  88.8 us (13%)
  between operations  14.3 us (2%)
  starting transfers between devices  12 us (2%)
  blocking collectives  12 us (2%)
    dot_general x16, matrix products, backward(): jnp.einsum('wkij,kswjc->swic', back_block, across, preferred_element_type...  78.1 us
    dot_general x16, matrix products, forward(): jnp.einsum('kswic,wkcd->swid', row_pass, column_block, preferred_element_...  63.2 us
    psum x1, waiting for transfers between devices, per_device(): gradient_total = lax.psum(gradient_flat, 'wave')  50.7 us
    mul x64, other arithmetic, stokes_model(): parameter_span[number] * unit_params[number]  45.4 us
    dynamic_update_slice x2, local copies, waits for them, and re-layouts, extend(): lax.dynamic_update_slice_in_dim(widened, lower_rim, radius + length, axis...  43.3 us
    dynamic_slice x16, local copies, waits for them, and re-layouts, backward(): back_block = lax.dynamic_slice_in_dim(row_back, first_wave, block_size, 0)  40.4 us
    ppermute x4, waiting for transfers between devices, passed_along(): return lax.ppermute(shard, axis, pairs)  38.1 us
    dynamic_slice x32, local copies, waits for them, and re-layouts, forward(): band_block = lax.dynamic_slice_in_dim(row_band, first_wave, block_size, 0)  36.4 us
  transfers between devices with their start and end apart: 5, of which 2 were waited for; matrix products, arithmetic and copies ran while one was open for 10% of the time, Pallas kernels for 0%

commit v1 on v0

v1 whole, which is shorter than its diff:
```python
import functools

import jax
import jax.numpy as jnp
from jax import lax
from jax.experimental import pallas as pl
from jax.experimental.pallas import tpu as pltpu
from jax.sharding import PartitionSpec as P

parameter_low = (0.2, 0.4, 2.0, -0.8, 0.4, 0.3, 0.0, 0.0, 0.0)
parameter_span = (0.4, 0.6, 18.0, 1.6, 0.8, 1.2, 1.5, 3.141592653589793, 3.141592653589793)
stokes_weight = (1.0, 9.0, 9.0, 4.0)
loss_scale = 0.03125
lanes = 128


def passed_along(shard, axis, by):
    count = lax.axis_size(axis)
    pairs = [(i, i + by) for i in range(count) if 0 <= i + by < count]
    return lax.ppermute(shard, axis, pairs)


def swapped(shard, axis, step):
    count = lax.axis_size(axis)
    return lax.ppermute(shard, axis, [(i, i ^ step) for i in range(count)])


def physical_of(unit_params):
    return [
        parameter_low[number] + parameter_span[number] * unit_params[number] for number in range(9)
    ]


def inverse(value):
    guess = pl.reciprocal(value, approx=True)
    return guess * (2.0 - value * guess)


def circulant(taps, rows):
    wide = jnp.broadcast_to(taps, (rows, lanes))
    return pltpu.roll(wide, 0, 1, stride=1, stride_axis=0)


def kernel(
    grid_ref,
    const_ref,
    mask_ref,
    observed_ref,
    taps_ref,
    out_ref,
    model_ref,
    saved_ref,
    adjoint_ref,
    row_ref,
    back_ref,
    column_ref,
    pass_ref,
    residual_ref,
    across_ref,
):
    step = pl.program_id(0)
    steps = pl.num_programs(0)
    ranks = taps_ref.shape[1]
    stokes, _, rows, columns = observed_ref.shape
    wide = const_ref.shape[1]

    def model_chunk(slot, level, row, column):
        here = (pl.ds(row, 16), pl.ds(column, lanes))
        scale, shift, split, lin, tot, circ, zero, slope, cos2, sin2 = (
            const_ref[(number,) + here] for number in range(10)
        )
        z0 = level * scale - shift
        z1 = z0 - split
        z2 = z0 + split
        p0 = inverse(1.0 + z0 * z0)
        p1 = inverse(1.0 + z1 * z1)
        p2 = inverse(1.0 + z2 * z2)
        both = p1 + p2
        differ = p2 - p1
        absorb = 1.0 + lin * p0 + tot * both
        linear = lin * (p0 - 0.5 * both)
        circular = circ * differ
        inv = inverse(absorb * absorb - linear * linear - circular * circular)
        ratio = slope * inv
        polar = ratio * linear
        models = (zero + ratio * absorb, -(polar * cos2), -(polar * sin2), -(ratio * circular))
        for number in range(stokes):
            model_ref[(slot, number) + here] = models[number].astype(jnp.bfloat16)
        kept = (p0, both, differ, z0 * p0 * p0, z1 * p1 * p1, z2 * p2 * p2, absorb, inv)
        for number in range(8):
            saved_ref[(slot, number) + here] = kept[number]

    def pull_chunk(slot, level, row, column):
        here = (pl.ds(row, 16), pl.ds(column, lanes))
        p0, both, differ, y0, y1, y2, absorb, inv = (
            saved_ref[(slot, number) + here] for number in range(8)
        )
        lin, tot, circ = (const_ref[(number,) + here] for number in (3, 4, 5))
        slope, cos2, sin2 = (const_ref[(number,) + here] for number in (7, 8, 9))
        h0, h1, h2, h3 = (adjoint_ref[(slot, number) + here] for number in range(4))
        part = p0 - 0.5 * both
        linear = lin * part
        circular = circ * differ
        ratio = slope * inv
        along = h1 * cos2 + h2 * sin2
        turned = h2 * cos2 - h1 * sin2
        term = (h0 * absorb - along * linear - h3 * circular) * inv
        twice = term + term
        g_absorb = ratio * (h0 - twice * absorb)
        g_linear = ratio * (twice * linear - along)
        g_circular = ratio * (twice * circular - h3)
        g_both = tot * g_absorb - (0.5 * lin) * g_linear
        g_differ = circ * g_circular
        d1 = y1 * (g_both - g_differ)
        d2 = y2 * (g_both + g_differ)
        dz = y0 * (lin * (g_absorb + g_linear)) + d1 + d2
        sums = (
            h0,
            term,
            ratio * linear * turned,
            g_absorb * p0 + g_linear * part,
            g_absorb * both,
            g_circular * differ,
            dz,
            level * dz,
            d2 - d1,
        )
        for number in range(9):
            out_ref[(number,) + here] += sums[number]

    chunks = [(row, column) for row in range(0, wide, 16) for column in range(0, columns, lanes)]

    def chunk_loop(body, slot, level):
        def one(number, carry):
            row = pl.multiple_of(number * 16, 16)
            for column in range(0, columns, lanes):
                body(slot, level, row, column)
            return carry

        lax.fori_loop(0, wide // 16, one, 0)

    @pl.when(step == 0)
    def _():
        out_ref[...] = jnp.zeros_like(out_ref)
        saved_ref[1] = jnp.zeros(saved_ref.shape[1:], jnp.float32)
        adjoint_ref[1] = jnp.zeros(adjoint_ref.shape[1:], jnp.float32)
        model_ref[...] = jnp.zeros_like(model_ref)
        across_ref[...] = jnp.zeros_like(across_ref)
        column_ref[...] = jnp.zeros_like(column_ref)
        chunk_loop(model_chunk, 0, grid_ref[0])

    def tables(slot, rank):
        source = lax.broadcasted_iota(jnp.int32, (lanes, lanes), 0)
        target = lax.broadcasted_iota(jnp.int32, (lanes, lanes), 1)
        taps = taps_ref[slot, rank : rank + 1, :]
        ring = circulant(taps[:, :lanes], lanes)
        near = jnp.where(jnp.abs(source - target) <= 64, ring, 0.0).astype(jnp.bfloat16)
        after = jnp.where(source - target > 64, ring, 0.0).astype(jnp.bfloat16)
        before = jnp.where(target - source > 64, ring, 0.0).astype(jnp.bfloat16)
        base = rank * columns
        for block in range(columns // lanes):
            place = base + block * lanes
            column_ref[pl.ds(place, lanes), pl.ds(block * lanes, lanes)] = near
            if block > 0:
                column_ref[pl.ds(place, lanes), pl.ds((block - 1) * lanes, lanes)] = before
                column_ref[pl.ds(place - lanes, lanes), pl.ds(block * lanes, lanes)] = after
        ring = circulant(taps[:, lanes : 2 * lanes], rows)
        ahead = target[:rows] >= source[:rows]
        row_ref[pl.ds(rank * rows, rows), :lanes] = jnp.where(ahead, ring, 0.0).astype(jnp.bfloat16)
        row_ref[pl.ds(rank * rows, rows), lanes:] = jnp.where(ahead, 0.0, ring).astype(jnp.bfloat16)
        ring = circulant(taps[:, 2 * lanes :], lanes)
        inside = target <= source
        at = pl.ds(rank * lanes, lanes)
        back_ref[:lanes, at] = jnp.where(inside, ring, 0.0).astype(jnp.bfloat16)
        back_ref[lanes:, at] = jnp.where(inside, 0.0, ring)[: wide - lanes].astype(jnp.bfloat16)

    def row_piece(slot, number):
        product = jnp.dot(
            row_ref[...], model_ref[slot, number], preferred_element_type=jnp.float32
        ).astype(jnp.bfloat16)
        for rank in range(ranks):
            pass_ref[pl.ds(number * rows, rows), pl.ds(rank * columns, columns)] = product[
                rank * rows : (rank + 1) * rows
            ]

    def blur_piece(slot):
        blurred = jnp.dot(pass_ref[...], column_ref[...], preferred_element_type=jnp.float32)
        for number in range(stokes):
            seen = observed_ref[number, slot].astype(jnp.float32)
            gap = blurred[number * rows : (number + 1) * rows] - seen
            weighted = (stokes_weight[number] * mask_ref[...]) * gap
            residual_ref[pl.ds(number * rows, rows), :] = weighted.astype(jnp.bfloat16)

    def across_piece(rank):
        product = lax.dot_general(
            residual_ref[...],
            column_ref[pl.ds(rank * columns, columns), :],
            (((1,), (1,)), ((), ())),
            preferred_element_type=jnp.float32,
        ).astype(jnp.bfloat16)
        for number in range(stokes):
            across_ref[pl.ds(rank * lanes, rows), pl.ds(number * columns, columns)] = product[
                number * rows : (number + 1) * rows
            ]

    def adjoint_piece(slot, number):
        adjoint_ref[slot, number] = jnp.dot(
            back_ref[...],
            across_ref[:, pl.ds(number * columns, columns)],
            preferred_element_type=jnp.float32,
        )

    for slot in (0, 1):
        other = 1 - slot
        now = 2 * step + slot
        before_level = grid_ref[jnp.maximum(now - 1, 0)]
        after_level = grid_ref[now + 1]
        matrix = [functools.partial(tables, slot, rank) for rank in range(ranks)]
        matrix += [functools.partial(row_piece, slot, number) for number in range(stokes)]
        matrix += [functools.partial(blur_piece, slot)]
        matrix += [functools.partial(across_piece, rank) for rank in range(ranks)]
        matrix += [functools.partial(adjoint_piece, slot, number) for number in range(stokes)]
        vector = [functools.partial(pull_chunk, other, before_level, *at) for at in chunks]
        vector += [functools.partial(model_chunk, other, after_level, *at) for at in chunks]
        done = 0
        for number, piece in enumerate(matrix):
            piece()
            until = (number + 1) * len(vector) // len(matrix)
            for work in vector[done:until]:
                work()
            done = until

    @pl.when(step == steps - 1)
    def _():
        chunk_loop(pull_chunk, 1, grid_ref[2 * steps - 1])


def wave_sums(grid, consts, mask, observed, taps):
    stokes, waves, rows, columns = observed.shape
    ranks = taps.shape[1]
    wide = consts.shape[1]
    return pl.pallas_call(
        kernel,
        grid=(waves // 2,),
        out_shape=jax.ShapeDtypeStruct((9, wide, columns), jnp.float32),
        in_specs=[
            pl.BlockSpec(memory_space=pltpu.SMEM),
            pl.BlockSpec(consts.shape, lambda i: (0, 0, 0)),
            pl.BlockSpec(mask.shape, lambda i: (0, 0)),
            pl.BlockSpec((stokes, 2, rows, columns), lambda i: (0, i, 0, 0)),
            pl.BlockSpec((2,) + taps.shape[1:], lambda i: (i, 0, 0)),
        ],
        out_specs=pl.BlockSpec((9, wide, columns), lambda i: (0, 0, 0)),
        scratch_shapes=[
            pltpu.VMEM((2, stokes, 2 * lanes, columns), jnp.bfloat16),
            pltpu.VMEM((2, 8, wide, columns), jnp.float32),
            pltpu.VMEM((2, stokes, wide, columns), jnp.float32),
            pltpu.VMEM((ranks * rows, 2 * lanes), jnp.bfloat16),
            pltpu.VMEM((wide, ranks * lanes), jnp.bfloat16),
            pltpu.VMEM((ranks * columns, columns), jnp.bfloat16),
            pltpu.VMEM((stokes * rows, ranks * columns), jnp.bfloat16),
            pltpu.VMEM((stokes * rows, columns), jnp.bfloat16),
            pltpu.VMEM((ranks * lanes, stokes * columns), jnp.bfloat16),
        ],
        compiler_params=pltpu.CompilerParams(vmem_limit_bytes=48 * 1024 * 1024),
    )(grid, consts, mask, observed, taps)


def pixel_constants(params, live):
    zero, slope, strength, doppler, width, damping, split, incline, azimuth = physical_of(params)
    scale = 1.0 / (width * damping)
    cosine = jnp.cos(incline)
    sine = jnp.sin(incline)
    return jnp.stack(
        [
            scale,
            doppler * scale,
            split * scale,
            0.5 * strength * sine * sine,
            0.25 * strength * (1.0 + cosine * cosine),
            0.5 * strength * cosine,
            zero * live,
            slope * live,
            jnp.cos(2.0 * azimuth),
            jnp.sin(2.0 * azimuth),
        ]
    )


def unit_gradient(params, sums):
    _, _, strength, doppler, width, damping, split, incline, _ = physical_of(params)
    scale = 1.0 / (width * damping)
    cosine = jnp.cos(incline)
    sine = jnp.sin(incline)
    dz, dz_level, d_split = -2.0 * sums[6], -2.0 * sums[7], -2.0 * sums[8]
    d_scale = dz_level - doppler * dz + split * d_split
    physical = [
        sums[0],
        sums[1],
        0.5 * sine * sine * sums[3]
        + 0.25 * (1.0 + cosine * cosine) * sums[4]
        + 0.5 * cosine * sums[5],
        -scale * dz,
        -d_scale * scale / width,
        -d_scale * scale / damping,
        scale * d_split,
        strength * sine * (cosine * sums[3] - 0.5 * cosine * sums[4] - 0.5 * sums[5]),
        -2.0 * sums[2],
    ]
    return jnp.stack([parameter_span[number] * physical[number] for number in range(9)])


def per_device(unit_params, observed, psf_rows, psf_cols, pixel_mask, strip_lengths):
    stokes_count, wave_count, capacity, columns = observed.shape
    ranks, tap_count = psf_rows.shape[1:]
    radius = tap_count // 2
    wave_pos = lax.axis_index("wave")
    wave_total = lax.axis_size("wave")
    strip_pos = lax.axis_index("strip")
    strip_total = lax.axis_size("strip")
    length = strip_lengths[0]
    share = capacity // wave_total
    mine = unit_params.reshape(9, share, columns)

    others = [(wave_pos ^ step, swapped(mine, "wave", step)) for step in range(1, wave_total)]
    own = jnp.zeros((9, capacity, columns), jnp.float32)
    for place, block in [(wave_pos, mine)] + others:
        own = lax.dynamic_update_slice_in_dim(own, block, place * share, 1)
    tail = lax.dynamic_slice_in_dim(own, length - radius, radius, 1)
    upper = passed_along(tail, "strip", 1)
    lower = passed_along(own[:, :radius], "strip", -1)
    params = jnp.concatenate([upper, own, jnp.zeros_like(upper)], axis=1)
    params = lax.dynamic_update_slice_in_dim(params, lower, radius + length, 1)

    index = jnp.arange(capacity + 2 * radius, dtype=jnp.int32)
    live = (
        (index < radius) & (strip_pos > 0)
        | (index >= radius) & (index < radius + length)
        | (index >= radius + length)
        & (index < 2 * radius + length)
        & (strip_pos < strip_total - 1)
    )
    consts = pixel_constants(params, live.astype(jnp.float32)[:, None])
    rows_live = (jnp.arange(capacity, dtype=jnp.int32) < length)[:, None]
    mask = loss_scale * pixel_mask.astype(jnp.float32) * rows_live

    levels = (wave_pos * wave_count + jnp.arange(wave_count + 2, dtype=jnp.int32)).astype(
        jnp.float32
    )
    grid = -3.0 + 6.0 * levels / (wave_count * wave_total - 1)

    rows32 = psf_rows.astype(jnp.float32)
    cols32 = psf_cols.astype(jnp.float32)[:, :, ::-1]
    back32 = rows32[:, :, ::-1]
    gap = jnp.zeros((wave_count, ranks, lanes - tap_count), jnp.float32)
    taps = jnp.concatenate(
        [
            cols32[:, :, radius:],
            gap,
            cols32[:, :, :radius],
            rows32,
            gap,
            back32[:, :, tap_count - 1 :],
            gap,
            back32[:, :, : tap_count - 1],
        ],
        axis=2,
    )
    sums = wave_sums(grid, consts, mask, observed, taps)

    from_lower = passed_along(sums[:, :radius], "strip", -1)
    from_upper = passed_along(
        lax.dynamic_slice_in_dim(sums, radius + length, radius, 1), "strip", 1
    )
    total = jnp.where(rows_live, sums[:, radius : radius + capacity], 0.0)
    total = jnp.concatenate([total[:, :radius] + from_upper, total[:, radius:]], axis=1)
    ending = lax.dynamic_slice_in_dim(total, length - radius, radius, 1) + from_lower
    total = lax.dynamic_update_slice_in_dim(total, ending, length - radius, 1)

    def part(place):
        return lax.dynamic_slice_in_dim(total, place * share, share, 1)

    arrived = [swapped(part(wave_pos ^ step), "wave", step) for step in range(1, wave_total)]
    mine_sums = functools.reduce(jnp.add, arrived, part(wave_pos))
    return unit_gradient(mine, mine_sums).reshape(unit_params.shape)


def solution(mesh):
    return jax.shard_map(
        per_device,
        mesh=mesh,
        in_specs=(
            P(None, "strip", "wave"),
            P(None, "wave", "strip", None),
            P("wave", None, None),
            P("wave", None, None),
            P("strip", None),
            P("strip"),
        ),
        out_specs=P(None, "strip", "wave"),
        check_vma=False,
    )
```

time: 691 us -> 189 us (0.27)
  other arithmetic: 206 us -> 6.54 us
  local copies, waits for them, and re-layouts: 182 us -> 9 us
  matrix products: 168 us -> 0 us
  Pallas kernels: 0 us -> 127 us
  waiting for transfers between devices: 88.8 us -> 27.9 us
  between operations: 14.3 us -> 1.26 us
  blocking collectives: 12 us -> 0 us
    dot_general x35 -> x0, matrix products: 168 us -> none  [the longest x16 78.1 us: backward(): jnp.einsum('wkij,kswjc->swic', back_block, across, preferred_element_type...]
    pallas_call x0 -> x1, Pallas kernels: none -> 127 us  [wave_sums(): pl.pallas_call(kernel, grid=(waves // 2,), out_shape=jax.ShapeDtypeStruct...]
    dynamic_slice x66 -> x1, local copies, waits for them, and re-layouts: 79.7 us -> 0.06 us  [part(): return lax.dynamic_slice_in_dim(total, place * share, share, 1)]
    mul x129 -> x5, other arithmetic: 71 us -> 0.15 us  [the longest x2 0.08 us: per_device(): mask = loss_scale * pixel_mask.astype(jnp.float32) * rows_live]
    dynamic_update_slice x18 -> x5, local copies, waits for them, and re-layouts: 58.5 us -> 4.56 us  [the longest x1 2.29 us: per_device(): total = lax.dynamic_update_slice_in_dim(total, ending, length - radius, 1)]
    psum x1 -> x0, waiting for transfers between devices: 50.7 us -> none  [per_device(): gradient_total = lax.psum(gradient_flat, 'wave')]
    add x19 -> x5, other arithmetic: 41.1 us -> 1.38 us  [the longest x1 1.15 us: physical_of(): parameter_low[number] + parameter_span[number] * unit_params[number]]
    reduce_sum x64 -> x0, other arithmetic: 32 us -> none  [the longest x16 16 us: stokes_model(): linear_cosine = linear * jnp.cos(2.0 * azimuth)]
  transfers between devices with their start and end apart: 5 -> 10, of which waited for: 2 -> 9; matrix products, arithmetic and copies ran while one was open for 10% -> 2% of each run, Pallas kernels for 0% -> 0%
where the time goes in v1:
time: 189 us
  Pallas kernels  127 us (67%)
  waiting for transfers between devices  27.9 us (15%)
  starting transfers between devices  17.1 us (9%)
  local copies, waits for them, and re-layouts  9 us (5%)
  other arithmetic  6.54 us (3%)
    pallas_call x1, Pallas kernels, wave_sums(): pl.pallas_call(kernel, grid=(waves // 2,), out_shape=jax.ShapeDtypeStruct...  127 us
    ppermute x6, waiting for transfers between devices, swapped(): return lax.ppermute(shard, axis, [(i, i ^ step) for i in range(count)])  17.7 us
    ppermute x4, starting transfers between devices, passed_along(): return lax.ppermute(shard, axis, pairs)  11.7 us
    ppermute x4, waiting for transfers between devices, passed_along(): return lax.ppermute(shard, axis, pairs)  10.2 us
    ppermute x6, starting transfers between devices, swapped(): return lax.ppermute(shard, axis, [(i, i ^ step) for i in range(count)])  5.43 us
    unnamed x10, other arithmetic  4.05 us
  transfers between devices with their start and end apart: 10, of which 9 were waited for; matrix products, arithmetic and copies ran while one was open for 2% of the time, Pallas kernels for 0%

profile of v1, /device:TPU:17, one launch (start us, length us, event | category | flops | bytes accessed | tf_op | source)
XLA Modules:
  0.0 189.1 jit_solution(301984885120302834)
XLA Ops:
  0.0 1.5 reduce
  1.5 0.1 copy.7
  1.6 0.1 broadcast_in_dim.22
  1.7 0.0 copy-start.3
  1.7 0.0 copy-start.1
  1.7 1.3 collective-permute-start
  3.0 1.2 collective-permute-start.1
  4.3 0.2 collective-permute-start.2
  5.1 0.0 copy-start
  5.2 2.9 %collective-permute-done = f32[9,24,256]{2,1,0:T(8,128)S(1)} collective-permute-done((f32[9,24,256]{2,1,0:T(8,128)S(1)}, f32[9,24,256]{2,1,0:T(8,128)S(1)}, u32[]{:S(2)}, u32[]{:S(2)}) %collective-permute-start) | collective-permute-done | bytes 221216 | tf_op jit(solution)/shard_map/ppermute | solution.py:25
  8.1 0.9 collective-permute-done.1
  9.0 4.8 %collective-permute-done.2 = f32[9,24,256]{2,1,0:T(8,128)S(1)} collective-permute-done((f32[9,24,256]{2,1,0:T(8,128)S(1)}, f32[9,24,256]{2,1,0:T(8,128)S(1)}, u32[]{:S(2)}, u32[]{:S(2)}) %collective-permute-start.2) | collective-permute-done | bytes 221216 | tf_op jit(solution)/shard_map/ppermute | solution.py:25
  13.9 0.8 fusion.30
  14.6 4.9 %collective-permute-start.3 = (f32[9,32,256]{2,1,0:T(8,128)S(1)}, f32[9,32,256]{2,1,0:T(8,128)S(1)}, u32[]{:S(2)}, u32[]{:S(2)}) collective-permute-start(f32[9,32,256]{2,1,0:T(8,128)S(1)} %get-tuple-element.20), channel_id=1, source_target_pairs={{0,1},{1,2},{2,3},{3,4},{4,5},{5,6},{6,7},{8,9},{9,10},{10,11},{11... | collective-permute-start | bytes 884744 | tf_op jit(solution)/shard_map/ppermute | solution.py:20
  19.5 0.0 copy-done.3
  19.5 0.1 convert_multiply_fusion.mask_ref
  19.6 1.9 %collective-permute-start.4 = (f32[9,32,256]{2,1,0:T(8,128)}, f32[9,32,256]{2,1,0:T(8,128)S(1)}, u32[]{:S(2)}, u32[]{:S(2)}) collective-permute-start(f32[9,32,256]{2,1,0:T(8,128)} %get-tuple-element.19), channel_id=1, source_target_pairs={{1,0},{2,1},{3,2},{4,3},{5,4},{6,5},{7,6},{9,8},{10,9},{11,10},{12... | collective-permute-start | bytes 884744 | tf_op jit(solution)/shard_map/ppermute | solution.py:20
  21.6 0.0 copy-done.1
  21.6 0.1 slice.165
  21.7 0.0 copy-done
  21.7 0.1 slice.167
  21.8 0.2 slice.129
  22.0 0.2 slice.131
  22.2 0.2 slice.134
  22.5 0.8 concatenate.11.taps_ref
  23.3 0.0 collective-permute-done.3
  23.3 0.2 maximum_maximum_fusion
  23.5 4.4 %collective-permute-done.4 = f32[9,32,256]{2,1,0:T(8,128)S(1)} collective-permute-done((f32[9,32,256]{2,1,0:T(8,128)}, f32[9,32,256]{2,1,0:T(8,128)S(1)}, u32[]{:S(2)}, u32[]{:S(2)}) %collective-permute-start.4) | collective-permute-done | bytes 294944 | tf_op jit(solution)/shard_map/ppermute | solution.py:20
  27.9 2.2 %dynamic_update_slice.22 = f32[9,160,256]{2,1,0:T(8,128)S(1)} dynamic-update-slice(f32[9,160,256]{2,1,0:T(8,128)S(1)} %maximum_maximum_fusion, f32[9,32,256]{2,1,0:T(8,128)S(1)} %collective-permute-done.4, s32[]{:T(128)} %constant.41.clone.1, s32[]{:T(128)S(6)} %select_n.34, s32[]{:T(128)} %constant.41.clone.1) | dynamic-update-slice | bytes 589828 | tf_op jit(solution)/shard_map/dynamic_update_slice | solution.py:333
  30.1 0.1 fusion.14
  30.2 0.1 fusion.11
  30.3 0.6 fusion.2
  30.9 0.6 multiply_dynamic-update-slice_fusion.1
  31.4 0.6 multiply_dynamic-update-slice_fusion
  32.0 0.1 fusion.8
  32.1 0.1 fusion.5
  32.2 0.5 cosine_dynamic-update-slice_fusion
  32.7 0.5 sine_dynamic-update-slice_fusion.const_ref
  33.3 127.3 %shard_map.64 = f32[9,160,256]{2,1,0:T(8,128)S(1)} custom-call(f32[66]{0:T(128)S(1)} %multiply_add_fusion.grid_ref, f32[10,160,256]{2,1,0:T(8,128)S(1)} %sine_dynamic-update-slice_fusion.const_ref, f32[96,256]{1,0:T(8,128)S(1)} %convert_multiply_fusion.mask_ref, bf16[4,64,96,256]{3,2,1,0:T(8,128)(2,1)} %observed_ref.1, f32[64,4,384]{2,1,0:T(4,128)S(1)} %concatenate.11.taps_ref), custom_call_target="tpu_custom_call" | custom-call | tf_op jit(solution)/shard_map/pallas_call | solution.py:242
  160.6 0.1 fusion.29
  160.6 2.8 %collective-permute-start.5 = (f32[9,32,256]{2,1,0:T(8,128)S(1)}, f32[9,32,256]{2,1,0:T(8,128)S(1)}, u32[]{:S(2)}, u32[]{:S(2)}) collective-permute-start(f32[9,32,256]{2,1,0:T(8,128)S(1)} %get-tuple-element.15), channel_id=1, source_target_pairs={{0,1},{1,2},{2,3},{3,4},{4,5},{5,6},{6,7},{8,9},{9,10},{10,11},{11... | collective-permute-start | bytes 884744 | tf_op jit(solution)/shard_map/ppermute | solution.py:20
  163.4 0.1 slice_select_fusion
  163.6 2.1 %collective-permute-start.6 = (f32[9,32,256]{2,1,0:T(8,128)S(1)}, f32[9,32,256]{2,1,0:T(8,128)S(1)}, u32[]{:S(2)}, u32[]{:S(2)}) collective-permute-start(f32[9,32,256]{2,1,0:T(8,128)S(1)} %get-tuple-element.14), channel_id=1, source_target_pairs={{1,0},{2,1},{3,2},{4,3},{5,4},{6,5},{7,6},{9,8},{10,9},{11,10},{12... | collective-permute-start | bytes 884744 | tf_op jit(solution)/shard_map/ppermute | solution.py:20
  165.7 1.3 collective-permute-done.5
  167.1 0.1 pad_maximum_fusion
  167.2 0.0 copy-start.2
  167.2 4.5 %collective-permute-done.6 = f32[9,32,256]{2,1,0:T(8,128)S(1)} collective-permute-done((f32[9,32,256]{2,1,0:T(8,128)S(1)}, f32[9,32,256]{2,1,0:T(8,128)S(1)}, u32[]{:S(2)}, u32[]{:S(2)}) %collective-permute-start.6) | collective-permute-done | bytes 294944 | tf_op jit(solution)/shard_map/ppermute | solution.py:20
  171.6 0.1 fusion.1
  171.8 2.3 %dynamic_update_slice.23 = f32[9,96,256]{2,1,0:T(8,128)S(1)} dynamic-update-slice(f32[9,96,256]{2,1,0:T(8,128)S(1)} %pad_maximum_fusion, f32[9,32,256]{2,1,0:T(8,128)S(1)} %fusion.1, s32[]{:T(128)} %constant.41.clone.1, s32[]{:T(128)S(6)} %select_n.33, s32[]{:T(128)} %constant.41.clone.1) | dynamic-update-slice | bytes 589828 | tf_op jit(solution)/shard_map/dynamic_update_slice | solution.py:378
  174.1 0.1 constant_dynamic-slice_fusion.2
  174.1 1.0 collective-permute-start.7
  175.1 0.6 collective-permute-start.8
  175.7 1.2 collective-permute-start.9
  176.8 0.0 copy-done.2
  176.8 1.1 add_reduce_fusion
  178.1 3.4 %collective-permute-done.7 = f32[9,24,256]{2,1,0:T(8,128)S(1)} collective-permute-done((f32[9,24,256]{2,1,0:T(8,128)S(1)}, f32[9,24,256]{2,1,0:T(8,128)S(1)}, u32[]{:S(2)}, u32[]{:S(2)}) %collective-permute-start.7) | collective-permute-done | bytes 221216 | tf_op jit(solution)/shard_map/ppermute | solution.py:25
  181.5 0.7 collective-permute-done.8
  182.2 5.0 %collective-permute-done.9 = f32[9,24,256]{2,1,0:T(8,128)S(1)} collective-permute-done((f32[9,24,256]{2,1,0:T(8,128)S(1)}, f32[9,24,256]{2,1,0:T(8,128)S(1)}, u32[]{:S(2)}, u32[]{:S(2)}) %collective-permute-start.9) | collective-permute-done | bytes 221216 | tf_op jit(solution)/shard_map/ppermute | solution.py:25
  187.2 0.1 add_add_fusion
  187.8 0.0 copy-start.4
  187.8 0.7 copy-done.4
  188.5 0.6 constant_dynamic-update-slice_fusion.1
  (43 shorter events, 0.7 us)
Async XLA Ops:
  1.7 17.8 %copy-start.3 = (s32[96,256]{1,0:T(8,128)S(1)}, s32[96,256]{1,0:T(8,128)}, u32[]{:S(2)}) copy-start(s32[96,256]{1,0:T(8,128)} %param.10) | copy-start | bytes 294916
  1.7 19.9 %copy-start.1 = (bf16[64,4,65]{2,1,0:T(4,128)(2,1)S(1)}, bf16[64,4,65]{2,1,0:T(4,128)(2,1)}, u32[]{:S(2)}) copy-start(bf16[64,4,65]{2,1,0:T(4,128)(2,1)} %param.9) | copy-start | bytes 99844
  1.7 6.4 %collective-permute-start = (f32[9,24,256]{2,1,0:T(8,128)S(1)}, f32[9,24,256]{2,1,0:T(8,128)S(1)}, u32[]{:S(2)}, u32[]{:S(2)}) collective-permute-start(f32[9,24,256]{2,1,0:T(8,128)S(1)} %get-tuple-element.21), channel_id=1, source_target_pairs={{0,8},{8,0},{16,24},{24,16},{1,9},{9,1},{17,25},{25,17},{2,10},{10... | collective-permute-start | bytes 663560 | tf_op jit(solution)/shard_map/ppermute | solution.py:25
  3.0 6.0 %collective-permute-start.1 = (f32[9,24,256]{2,1,0:T(8,128)S(1)}, f32[9,24,256]{2,1,0:T(8,128)S(1)}, u32[]{:S(2)}, u32[]{:S(2)}) collective-permute-start(f32[9,24,256]{2,1,0:T(8,128)S(1)} %get-tuple-element.21), channel_id=1, source_target_pairs={{0,16},{8,24},{16,0},{24,8},{1,17},{9,25},{17,1},{25,9},{2,18},{10... | collective-permute-start | bytes 663560 | tf_op jit(solution)/shard_map/ppermute | solution.py:25
  4.3 9.6 %collective-permute-start.2 = (f32[9,24,256]{2,1,0:T(8,128)S(1)}, f32[9,24,256]{2,1,0:T(8,128)S(1)}, u32[]{:S(2)}, u32[]{:S(2)}) collective-permute-start(f32[9,24,256]{2,1,0:T(8,128)S(1)} %get-tuple-element.21), channel_id=1, source_target_pairs={{0,24},{8,16},{16,8},{24,0},{1,25},{9,17},{17,9},{25,1},{2,26},{10... | collective-permute-start | bytes 663560 | tf_op jit(solution)/shard_map/ppermute | solution.py:25
  5.1 16.6 %copy-start = (bf16[64,4,65]{2,1,0:T(4,128)(2,1)S(1)}, bf16[64,4,65]{2,1,0:T(4,128)(2,1)}, u32[]{:S(2)}) copy-start(bf16[64,4,65]{2,1,0:T(4,128)(2,1)} %param.8) | copy-start | bytes 99844
  14.6 8.6 %collective-permute-start.3 = (f32[9,32,256]{2,1,0:T(8,128)S(1)}, f32[9,32,256]{2,1,0:T(8,128)S(1)}, u32[]{:S(2)}, u32[]{:S(2)}) collective-permute-start(f32[9,32,256]{2,1,0:T(8,128)S(1)} %get-tuple-element.20), channel_id=1, source_target_pairs={{0,1},{1,2},{2,3},{3,4},{4,5},{5,6},{6,7},{8,9},{9,10},{10,11},{11... | collective-permute-start | bytes 884744 | tf_op jit(solution)/shard_map/ppermute | solution.py:20
  19.6 8.3 %collective-permute-start.4 = (f32[9,32,256]{2,1,0:T(8,128)}, f32[9,32,256]{2,1,0:T(8,128)S(1)}, u32[]{:S(2)}, u32[]{:S(2)}) collective-permute-start(f32[9,32,256]{2,1,0:T(8,128)} %get-tuple-element.19), channel_id=1, source_target_pairs={{1,0},{2,1},{3,2},{4,3},{5,4},{6,5},{7,6},{9,8},{10,9},{11,10},{12... | collective-permute-start | bytes 884744 | tf_op jit(solution)/shard_map/ppermute | solution.py:20
  160.6 6.4 %collective-permute-start.5 = (f32[9,32,256]{2,1,0:T(8,128)S(1)}, f32[9,32,256]{2,1,0:T(8,128)S(1)}, u32[]{:S(2)}, u32[]{:S(2)}) collective-permute-start(f32[9,32,256]{2,1,0:T(8,128)S(1)} %get-tuple-element.15), channel_id=1, source_target_pairs={{0,1},{1,2},{2,3},{3,4},{4,5},{5,6},{6,7},{8,9},{9,10},{10,11},{11... | collective-permute-start | bytes 884744 | tf_op jit(solution)/shard_map/ppermute | solution.py:20
  163.6 8.0 %collective-permute-start.6 = (f32[9,32,256]{2,1,0:T(8,128)S(1)}, f32[9,32,256]{2,1,0:T(8,128)S(1)}, u32[]{:S(2)}, u32[]{:S(2)}) collective-permute-start(f32[9,32,256]{2,1,0:T(8,128)S(1)} %get-tuple-element.14), channel_id=1, source_target_pairs={{1,0},{2,1},{3,2},{4,3},{5,4},{6,5},{7,6},{9,8},{10,9},{11,10},{12... | collective-permute-start | bytes 884744 | tf_op jit(solution)/shard_map/ppermute | solution.py:20
  167.2 9.7 %copy-start.2 = (f32[9,1,6144]{2,1,0:T(1,128)S(1)}, f32[9,1,6144]{2,1,0:T(1,128)}, u32[]{:S(2)}) copy-start(f32[9,1,6144]{2,1,0:T(1,128)} %param.6) | copy-start | bytes 663556
  174.1 7.4 %collective-permute-start.7 = (f32[9,24,256]{2,1,0:T(8,128)S(1)}, f32[9,24,256]{2,1,0:T(8,128)S(1)}, u32[]{:S(2)}, u32[]{:S(2)}) collective-permute-start(f32[9,24,256]{2,1,0:T(8,128)S(1)} %get-tuple-element.16), channel_id=1, source_target_pairs={{0,8},{8,0},{16,24},{24,16},{1,9},{9,1},{17,25},{25,17},{2,10},{10... | collective-permute-start | bytes 663560 | tf_op jit(solution)/shard_map/ppermute | solution.py:25
  175.1 7.1 %collective-permute-start.8 = (f32[9,24,256]{2,1,0:T(8,128)S(1)}, f32[9,24,256]{2,1,0:T(8,128)S(1)}, u32[]{:S(2)}, u32[]{:S(2)}) collective-permute-start(f32[9,24,256]{2,1,0:T(8,128)S(1)} %get-tuple-element.18), channel_id=1, source_target_pairs={{0,16},{8,24},{16,0},{24,8},{1,17},{9,25},{17,1},{25,9},{2,18},{10... | collective-permute-start | bytes 663560 | tf_op jit(solution)/shard_map/ppermute | solution.py:25
  175.7 11.5 %collective-permute-start.9 = (f32[9,24,256]{2,1,0:T(8,128)S(1)}, f32[9,24,256]{2,1,0:T(8,128)S(1)}, u32[]{:S(2)}, u32[]{:S(2)}) collective-permute-start(f32[9,24,256]{2,1,0:T(8,128)S(1)} %get-tuple-element.17), channel_id=1, source_target_pairs={{0,24},{8,16},{16,8},{24,0},{1,25},{9,17},{17,9},{25,1},{2,26},{10... | collective-permute-start | bytes 663560 | tf_op jit(solution)/shard_map/ppermute | solution.py:25
  187.8 0.7 copy-start.4

commit v2 on v1

v2 whole, which is shorter than its diff:
```python
import functools

import jax
import jax.numpy as jnp
from jax import lax
from jax.experimental import pallas as pl
from jax.experimental.pallas import tpu as pltpu
from jax.sharding import PartitionSpec as P

parameter_low = (0.2, 0.4, 2.0, -0.8, 0.4, 0.3, 0.0, 0.0, 0.0)
parameter_span = (0.4, 0.6, 18.0, 1.6, 0.8, 1.2, 1.5, 3.141592653589793, 3.141592653589793)
stokes_weight = (1.0, 9.0, 9.0, 4.0)
loss_scale = 0.03125
lanes = 128


def passed_along(shard, axis, by):
    count = lax.axis_size(axis)
    pairs = [(i, i + by) for i in range(count) if 0 <= i + by < count]
    return lax.ppermute(shard, axis, pairs)


def swapped(shard, axis, step):
    count = lax.axis_size(axis)
    return lax.ppermute(shard, axis, [(i, i ^ step) for i in range(count)])


def physical_of(unit_params):
    return [
        parameter_low[number] + parameter_span[number] * unit_params[number] for number in range(9)
    ]


def inverse(value):
    guess = pl.reciprocal(value, approx=True)
    return guess * (2.0 - value * guess)


def circulant(taps, rows):
    wide = jnp.broadcast_to(taps, (rows, lanes))
    return pltpu.roll(wide, 0, 1, stride=1, stride_axis=0)


def kernel(
    grid_ref,
    const_ref,
    mask_ref,
    observed_ref,
    taps_ref,
    out_ref,
    model_ref,
    saved_ref,
    adjoint_ref,
    row_ref,
    back_ref,
    column_ref,
    pass_ref,
    residual_ref,
    across_ref,
):
    step = pl.program_id(0)
    steps = pl.num_programs(0)
    ranks = taps_ref.shape[1]
    stokes, _, rows, columns = observed_ref.shape
    wide = const_ref.shape[1]

    def model_chunk(pair, levels, row, column):
        here = (pl.ds(row, 16), pl.ds(column, lanes))
        scale, shift, split, lin, tot, circ, zero, slope, cos2, sin2 = (
            const_ref[(number,) + here] for number in range(10)
        )
        for slot, level in zip(pair, levels):
            z0 = level * scale - shift
            z1 = z0 - split
            z2 = z0 + split
            p0 = inverse(1.0 + z0 * z0)
            p1 = inverse(1.0 + z1 * z1)
            p2 = inverse(1.0 + z2 * z2)
            both = p1 + p2
            differ = p2 - p1
            absorb = 1.0 + lin * p0 + tot * both
            linear = lin * (p0 - 0.5 * both)
            circular = circ * differ
            inv = inverse(absorb * absorb - linear * linear - circular * circular)
            ratio = slope * inv
            polar = ratio * linear
            models = (zero + ratio * absorb, -(polar * cos2), -(polar * sin2), -(ratio * circular))
            for number in range(stokes):
                model_ref[(slot, number) + here] = models[number].astype(jnp.bfloat16)
            kept = (p0, both, differ, z0 * p0 * p0, z1 * p1 * p1, z2 * p2 * p2, absorb, inv)
            for number in range(8):
                saved_ref[(slot, number) + here] = kept[number]

    def pull_chunk(pair, levels, row, column):
        here = (pl.ds(row, 8), pl.ds(column, lanes))
        lin, tot, circ = (const_ref[(number,) + here] for number in (3, 4, 5))
        slope, cos2, sin2 = (const_ref[(number,) + here] for number in (7, 8, 9))
        totals = [out_ref[(number,) + here] for number in range(9)]
        for slot, level in zip(pair, levels):
            p0, both, differ, y0, y1, y2, absorb, inv = (
                saved_ref[(slot, number) + here] for number in range(8)
            )
            h0, h1, h2, h3 = (adjoint_ref[(slot, number) + here] for number in range(4))
            part = p0 - 0.5 * both
            linear = lin * part
            circular = circ * differ
            ratio = slope * inv
            along = h1 * cos2 + h2 * sin2
            turned = h2 * cos2 - h1 * sin2
            term = (h0 * absorb - along * linear - h3 * circular) * inv
            twice = term + term
            g_absorb = ratio * (h0 - twice * absorb)
            g_linear = ratio * (twice * linear - along)
            g_circular = ratio * (twice * circular - h3)
            g_both = tot * g_absorb - (0.5 * lin) * g_linear
            g_differ = circ * g_circular
            d1 = y1 * (g_both - g_differ)
            d2 = y2 * (g_both + g_differ)
            dz = y0 * (lin * (g_absorb + g_linear)) + d1 + d2
            sums = (
                h0,
                term,
                ratio * linear * turned,
                g_absorb * p0 + g_linear * part,
                g_absorb * both,
                g_circular * differ,
                dz,
                level * dz,
                d2 - d1,
            )
            totals = [total + added for total, added in zip(totals, sums)]
        for number in range(9):
            out_ref[(number,) + here] = totals[number]

    def tables(slot, wave, rank):
        source = lax.broadcasted_iota(jnp.int32, (lanes, lanes), 0)
        target = lax.broadcasted_iota(jnp.int32, (lanes, lanes), 1)
        taps = taps_ref[wave, rank : rank + 1, :]
        ring = circulant(taps[:, :lanes], lanes)
        near = jnp.where(jnp.abs(source - target) <= 64, ring, 0.0).astype(jnp.bfloat16)
        after = jnp.where(source - target > 64, ring, 0.0).astype(jnp.bfloat16)
        before = jnp.where(target - source > 64, ring, 0.0).astype(jnp.bfloat16)
        base = rank * columns
        for block in range(columns // lanes):
            place = base + block * lanes
            column_ref[slot, pl.ds(place, lanes), pl.ds(block * lanes, lanes)] = near
            if block > 0:
                column_ref[slot, pl.ds(place, lanes), pl.ds((block - 1) * lanes, lanes)] = before
                column_ref[slot, pl.ds(place - lanes, lanes), pl.ds(block * lanes, lanes)] = after
        ring = circulant(taps[:, lanes : 2 * lanes], rows)
        ahead = target[:rows] >= source[:rows]
        at = pl.ds(rank * rows, rows)
        row_ref[slot, at, :lanes] = jnp.where(ahead, ring, 0.0).astype(jnp.bfloat16)
        row_ref[slot, at, lanes:] = jnp.where(ahead, 0.0, ring).astype(jnp.bfloat16)
        ring = circulant(taps[:, 2 * lanes :], lanes)
        inside = target <= source
        at = pl.ds(rank * lanes, lanes)
        back_ref[slot, :lanes, at] = jnp.where(inside, ring, 0.0).astype(jnp.bfloat16)
        rest = jnp.where(inside, 0.0, ring)[: wide - lanes]
        back_ref[slot, lanes:, at] = rest.astype(jnp.bfloat16)

    def row_piece(slot, number):
        product = jnp.dot(
            row_ref[slot], model_ref[slot, number], preferred_element_type=jnp.float32
        ).astype(jnp.bfloat16)
        for rank in range(ranks):
            pass_ref[slot % 2, pl.ds(number * rows, rows), pl.ds(rank * columns, columns)] = (
                product[rank * rows : (rank + 1) * rows]
            )

    def blur_piece(slot):
        blurred = jnp.dot(
            pass_ref[slot % 2], column_ref[slot], preferred_element_type=jnp.float32
        )
        for number in range(stokes):
            seen = observed_ref[number, slot].astype(jnp.float32)
            gap = blurred[number * rows : (number + 1) * rows] - seen
            weighted = (stokes_weight[number] * mask_ref[...]) * gap
            residual_ref[slot % 2, pl.ds(number * rows, rows), :] = weighted.astype(jnp.bfloat16)

    def across_piece(slot, rank):
        product = lax.dot_general(
            residual_ref[slot % 2],
            column_ref[slot, pl.ds(rank * columns, columns), :],
            (((1,), (1,)), ((), ())),
            preferred_element_type=jnp.float32,
        ).astype(jnp.bfloat16)
        for number in range(stokes):
            across_ref[slot % 2, pl.ds(rank * lanes, rows), pl.ds(number * columns, columns)] = (
                product[number * rows : (number + 1) * rows]
            )

    def adjoint_piece(slot, number):
        adjoint_ref[slot, number] = jnp.dot(
            back_ref[slot],
            across_ref[slot % 2, :, pl.ds(number * columns, columns)],
            preferred_element_type=jnp.float32,
        )

    def levels_at(wave):
        return [grid_ref[wave], grid_ref[wave + 1]]

    def strip_loop(body, height, pair, levels):
        def one(number, carry):
            row = pl.multiple_of(number * height, height)
            for column in range(0, columns, lanes):
                body(pair, levels, row, column)
            return carry

        lax.fori_loop(0, wide // height, one, 0)

    @pl.when(step == 0)
    def _():
        out_ref[...] = jnp.zeros_like(out_ref)
        saved_ref[2:] = jnp.zeros((2,) + saved_ref.shape[1:], jnp.float32)
        adjoint_ref[2:] = jnp.zeros((2,) + adjoint_ref.shape[1:], jnp.float32)
        model_ref[...] = jnp.zeros_like(model_ref)
        across_ref[...] = jnp.zeros_like(across_ref)
        column_ref[...] = jnp.zeros_like(column_ref)
        strip_loop(model_chunk, 16, (0, 1), levels_at(0))
        for slot in (0, 1):
            for rank in range(ranks):
                tables(slot, slot, rank)

    for half in (0, 1):
        pair = (2 * half, 2 * half + 1)
        other = (2 - 2 * half, 3 - 2 * half)
        now = 4 * step + 2 * half
        earlier = levels_at(jnp.maximum(now - 2, 0))
        later = levels_at(now + 2)
        matrix = []
        for number in range(stokes):
            matrix += [(1, functools.partial(row_piece, slot, number)) for slot in pair]
        matrix += [(4, functools.partial(blur_piece, slot)) for slot in pair]
        for rank in range(ranks):
            matrix += [(1, functools.partial(across_piece, slot, rank)) for slot in pair]
        for number in range(stokes):
            matrix += [(1, functools.partial(adjoint_piece, slot, number)) for slot in pair]
        vector = []
        for row in range(0, wide, 16):
            for column in range(0, columns, lanes):
                vector += [functools.partial(pull_chunk, other, earlier, row, column)]
                vector += [functools.partial(pull_chunk, other, earlier, row + 8, column)]
                vector += [functools.partial(model_chunk, other, later, row, column)]
        count = len(vector) // (2 * ranks)
        for number in range(2 * ranks):
            slot, rank = number % 2, number // 2
            vector.insert(
                (count + 1) * number, functools.partial(tables, other[slot], now + 2 + slot, rank)
            )
        whole = sum(weight for weight, _ in matrix)
        done = passed = 0
        for weight, piece in matrix:
            piece()
            passed += weight
            until = passed * len(vector) // whole
            for work in vector[done:until]:
                work()
            done = until

    @pl.when(step == steps - 1)
    def _():
        strip_loop(pull_chunk, 8, (2, 3), levels_at(4 * steps - 2))


def wave_sums(grid, consts, mask, observed, taps):
    stokes, waves, rows, columns = observed.shape
    ranks = taps.shape[1]
    wide = consts.shape[1]
    return pl.pallas_call(
        kernel,
        grid=(waves // 4,),
        out_shape=jax.ShapeDtypeStruct((9, wide, columns), jnp.float32),
        in_specs=[
            pl.BlockSpec(memory_space=pltpu.SMEM),
            pl.BlockSpec(consts.shape, lambda i: (0, 0, 0)),
            pl.BlockSpec(mask.shape, lambda i: (0, 0)),
            pl.BlockSpec((stokes, 4, rows, columns), lambda i: (0, i, 0, 0)),
            pl.BlockSpec(taps.shape, lambda i: (0, 0, 0)),
        ],
        out_specs=pl.BlockSpec((9, wide, columns), lambda i: (0, 0, 0)),
        scratch_shapes=[
            pltpu.VMEM((4, stokes, 2 * lanes, columns), jnp.bfloat16),
            pltpu.VMEM((4, 8, wide, columns), jnp.float32),
            pltpu.VMEM((4, stokes, wide, columns), jnp.float32),
            pltpu.VMEM((4, ranks * rows, 2 * lanes), jnp.bfloat16),
            pltpu.VMEM((4, wide, ranks * lanes), jnp.bfloat16),
            pltpu.VMEM((4, ranks * columns, columns), jnp.bfloat16),
            pltpu.VMEM((2, stokes * rows, ranks * columns), jnp.bfloat16),
            pltpu.VMEM((2, stokes * rows, columns), jnp.bfloat16),
            pltpu.VMEM((2, ranks * lanes, stokes * columns), jnp.bfloat16),
        ],
        compiler_params=pltpu.CompilerParams(vmem_limit_bytes=56 * 1024 * 1024),
    )(grid, consts, mask, observed, taps)


def pixel_constants(params, live):
    zero, slope, strength, doppler, width, damping, split, incline, azimuth = physical_of(params)
    scale = 1.0 / (width * damping)
    cosine = jnp.cos(incline)
    sine = jnp.sin(incline)
    return jnp.stack(
        [
            scale,
            doppler * scale,
            split * scale,
            0.5 * strength * sine * sine,
            0.25 * strength * (1.0 + cosine * cosine),
            0.5 * strength * cosine,
            zero * live,
            slope * live,
            jnp.cos(2.0 * azimuth),
            jnp.sin(2.0 * azimuth),
        ]
    )


def unit_gradient(params, sums):
    _, _, strength, doppler, width, damping, split, incline, _ = physical_of(params)
    scale = 1.0 / (width * damping)
    cosine = jnp.cos(incline)
    sine = jnp.sin(incline)
    dz, dz_level, d_split = -2.0 * sums[6], -2.0 * sums[7], -2.0 * sums[8]
    d_scale = dz_level - doppler * dz + split * d_split
    physical = [
        sums[0],
        sums[1],
        0.5 * sine * sine * sums[3]
        + 0.25 * (1.0 + cosine * cosine) * sums[4]
        + 0.5 * cosine * sums[5],
        -scale * dz,
        -d_scale * scale / width,
        -d_scale * scale / damping,
        scale * d_split,
        strength * sine * (cosine * sums[3] - 0.5 * cosine * sums[4] - 0.5 * sums[5]),
        -2.0 * sums[2],
    ]
    return jnp.stack([parameter_span[number] * physical[number] for number in range(9)])


def per_device(unit_params, observed, psf_rows, psf_cols, pixel_mask, strip_lengths):
    stokes_count, wave_count, capacity, columns = observed.shape
    ranks, tap_count = psf_rows.shape[1:]
    radius = tap_count // 2
    wave_pos = lax.axis_index("wave")
    wave_total = lax.axis_size("wave")
    strip_pos = lax.axis_index("strip")
    strip_total = lax.axis_size("strip")
    length = strip_lengths[0]
    share = capacity // wave_total
    mine = unit_params.reshape(9, share, columns)

    others = [(wave_pos ^ step, swapped(mine, "wave", step)) for step in range(1, wave_total)]
    own = jnp.zeros((9, capacity, columns), jnp.float32)
    for place, block in [(wave_pos, mine)] + others:
        own = lax.dynamic_update_slice_in_dim(own, block, place * share, 1)
    tail = lax.dynamic_slice_in_dim(own, length - radius, radius, 1)
    upper = passed_along(tail, "strip", 1)
    lower = passed_along(own[:, :radius], "strip", -1)
    index = jnp.arange(capacity + 2 * radius, dtype=jnp.int32)
    live = (
        (index < radius) & (strip_pos > 0)
        | (index >= radius) & (index < radius + length)
        | (index >= radius + length)
        & (index < 2 * radius + length)
        & (strip_pos < strip_total - 1)
    )
    wide = capacity + 2 * radius
    padded = jnp.pad(lower, ((0, 0), (capacity + radius, capacity - radius), (0, 0)))
    placed = lax.dynamic_slice_in_dim(padded, capacity - length, wide, 1)
    middle = jnp.pad(own, ((0, 0), (radius, radius), (0, 0)))
    first = jnp.pad(upper, ((0, 0), (0, wide - radius), (0, 0)))
    column_index = index[:, None]
    params = jnp.where(
        column_index < radius, first, jnp.where(column_index < radius + length, middle, placed)
    )
    consts = pixel_constants(params, live.astype(jnp.float32)[:, None])
    rows_live = (jnp.arange(capacity, dtype=jnp.int32) < length)[:, None]
    mask = loss_scale * pixel_mask.astype(jnp.float32) * rows_live

    levels = (wave_pos * wave_count + jnp.arange(wave_count + 4, dtype=jnp.int32)).astype(
        jnp.float32
    )
    grid = -3.0 + 6.0 * levels / (wave_count * wave_total - 1)

    rows32 = psf_rows.astype(jnp.float32)
    cols32 = psf_cols.astype(jnp.float32)[:, :, ::-1]
    back32 = rows32[:, :, ::-1]
    gap = jnp.zeros((wave_count, ranks, lanes - tap_count), jnp.float32)
    taps = jnp.concatenate(
        [
            cols32[:, :, radius:],
            gap,
            cols32[:, :, :radius],
            rows32,
            gap,
            back32[:, :, tap_count - 1 :],
            gap,
            back32[:, :, : tap_count - 1],
        ],
        axis=2,
    )
    taps = jnp.pad(taps, ((0, 4), (0, 0), (0, 0)))
    sums = wave_sums(grid, consts, mask, observed, taps)

    from_lower = passed_along(sums[:, :radius], "strip", -1)
    from_upper = passed_along(
        lax.dynamic_slice_in_dim(sums, radius + length, radius, 1), "strip", 1
    )
    total = jnp.where(rows_live, sums[:, radius : radius + capacity], 0.0)
    padded = jnp.pad(from_lower, ((0, 0), (capacity - radius,) * 2, (0, 0)))
    placed = lax.dynamic_slice_in_dim(padded, capacity - length, capacity, 1)
    total = total + placed + jnp.pad(from_upper, ((0, 0), (0, capacity - radius), (0, 0)))

    def part(place):
        return lax.dynamic_slice_in_dim(total, place * share, share, 1)

    arrived = [swapped(part(wave_pos ^ step), "wave", step) for step in range(1, wave_total)]
    mine_sums = functools.reduce(jnp.add, arrived, part(wave_pos))
    return unit_gradient(mine, mine_sums).reshape(unit_params.shape)


def solution(mesh):
    return jax.shard_map(
        per_device,
        mesh=mesh,
        in_specs=(
            P(None, "strip", "wave"),
            P(None, "wave", "strip", None),
            P("wave", None, None),
            P("wave", None, None),
            P("strip", None),
            P("strip"),
        ),
        out_specs=P(None, "strip", "wave"),
        check_vma=False,
    )
```

time: 189 us -> 163 us (0.86)
  Pallas kernels: 127 us -> 106 us
  waiting for transfers between devices: 27.9 us -> 21.1 us
  other arithmetic: 6.54 us -> 8.86 us
  local copies, waits for them, and re-layouts: 9 us -> 6.82 us
    pallas_call x1, Pallas kernels: 127 us -> 106 us  [wave_sums(): pl.pallas_call(kernel, grid=(waves // 4,), out_shape=jax.ShapeDtypeStruct...]
    dynamic_update_slice x2 -> x0, local copies, waits for them, and re-layouts: 4.5 us -> none  [the longest x1 2.29 us: per_device(): total = lax.dynamic_update_slice_in_dim(total, ending, length - radius, 1)]
    ppermute x4, waiting for transfers between devices: 10.2 us -> 6.33 us  [passed_along(): return lax.ppermute(shard, axis, pairs)]
    ppermute x6, waiting for transfers between devices: 17.7 us -> 14.7 us  [swapped(): return lax.ppermute(shard, axis, [(i, i ^ step) for i in range(count)])]
  transfers between devices with their start and end apart: 10 -> 10, of which waited for: 9 -> 8; matrix products, arithmetic and copies ran while one was open for 2% -> 3% of each run, Pallas kernels for 0% -> 0%
where the time goes in v2:
time: 163 us
  Pallas kernels  106 us (65%)
  waiting for transfers between devices  21.1 us (13%)
  starting transfers between devices  18.7 us (11%)
  other arithmetic  8.86 us (5%)
  local copies, waits for them, and re-layouts  6.82 us (4%)
    pallas_call x1, Pallas kernels, wave_sums(): pl.pallas_call(kernel, grid=(waves // 4,), out_shape=jax.ShapeDtypeStruct...  106 us
    ppermute x6, waiting for transfers between devices, swapped(): return lax.ppermute(shard, axis, [(i, i ^ step) for i in range(count)])  14.7 us
    ppermute x4, starting transfers between devices, passed_along(): return lax.ppermute(shard, axis, pairs)  13.3 us
    ppermute x4, waiting for transfers between devices, passed_along(): return lax.ppermute(shard, axis, pairs)  6.33 us
    ppermute x6, starting transfers between devices, swapped(): return lax.ppermute(shard, axis, [(i, i ^ step) for i in range(count)])  5.43 us
    unnamed x10, other arithmetic  4.08 us
  transfers between devices with their start and end apart: 10, of which 8 were waited for; matrix products, arithmetic and copies ran while one was open for 3% of the time, Pallas kernels for 0%

profile of v2, /device:TPU:17, one launch (start us, length us, event | category | flops | bytes accessed | tf_op | source)
XLA Modules:
  0.0 163.1 jit_solution(8205852615710057995)
XLA Ops:
  0.0 0.0 copy-start.2
  0.0 0.0 copy-start.1
  0.0 1.5 reduce
  1.5 0.1 copy.7
  1.6 0.1 broadcast_in_dim.34
  1.8 1.3 collective-permute-start
  3.0 1.2 collective-permute-start.1
  4.3 0.2 collective-permute-start.2
  4.5 0.0 copy-done.2
  4.5 0.1 slice.157
  4.6 0.0 copy-done.1
  4.6 0.1 slice.159
  5.4 0.2 slice.123
  5.6 0.2 slice.125
  5.8 0.2 slice.128
  6.0 0.8 concatenate.4
  6.8 0.0 copy-start.4
  6.8 0.8 pad.27.taps_ref
  7.7 0.5 multiply_add_fusion.grid_ref
  8.2 0.0 collective-permute-done
  8.2 0.8 collective-permute-done.1
  9.0 4.8 %collective-permute-done.2 = f32[9,24,256]{2,1,0:T(8,128)S(1)} collective-permute-done((f32[9,24,256]{2,1,0:T(8,128)S(1)}, f32[9,24,256]{2,1,0:T(8,128)S(1)}, u32[]{:S(2)}, u32[]{:S(2)}) %collective-permute-start.2) | collective-permute-done | bytes 221216 | tf_op jit(solution)/shard_map/ppermute | solution.py:25
  13.9 0.1 constant_dynamic-slice_fusion.4
  14.0 3.7 %collective-permute-start.4 = (f32[9,32,256]{2,1,0:T(8,128)S(1)}, f32[9,32,256]{2,1,0:T(8,128)S(1)}, u32[]{:S(2)}, u32[]{:S(2)}) collective-permute-start(f32[9,32,256]{2,1,0:T(8,128)S(1)} %get-tuple-element.20), channel_id=1, source_target_pairs={{1,0},{2,1},{3,2},{4,3},{5,4},{6,5},{7,6},{9,8},{10,9},{11,10},{12... | collective-permute-start | bytes 884744 | tf_op jit(solution)/shard_map/ppermute | solution.py:20
  17.7 3.3 %collective-permute-start.3 = (f32[9,32,256]{2,1,0:T(8,128)S(1)}, f32[9,32,256]{2,1,0:T(8,128)S(1)}, u32[]{:S(2)}, u32[]{:S(2)}) collective-permute-start(f32[9,32,256]{2,1,0:T(8,128)S(1)} %get-tuple-element.19), channel_id=1, source_target_pairs={{0,1},{1,2},{2,3},{3,4},{4,5},{5,6},{6,7},{8,9},{9,10},{10,11},{11... | collective-permute-start | bytes 884744 | tf_op jit(solution)/shard_map/ppermute | solution.py:20
  21.0 0.0 copy-done.4
  21.0 0.7 convert_multiply_fusion.mask_ref
  21.7 1.8 %collective-permute-done.4 = f32[9,32,256]{2,1,0:T(8,128)S(1)} collective-permute-done((f32[9,32,256]{2,1,0:T(8,128)S(1)}, f32[9,32,256]{2,1,0:T(8,128)S(1)}, u32[]{:S(2)}, u32[]{:S(2)}) %collective-permute-start.4) | collective-permute-done | bytes 294944 | tf_op jit(solution)/shard_map/ppermute | solution.py:20
  23.5 0.9 collective-permute-done.3
  24.4 0.4 fusion.1
  24.9 0.1 fusion.16
  24.9 0.1 fusion.13
  25.0 0.6 fusion.4
  25.6 0.6 multiply_dynamic-update-slice_fusion.1
  26.1 0.6 multiply_dynamic-update-slice_fusion
  26.7 0.1 fusion.10
  26.8 0.1 fusion.7
  26.9 0.5 cosine_dynamic-update-slice_fusion
  27.4 0.5 sine_dynamic-update-slice_fusion.const_ref
  28.0 0.0 copy-start
  28.0 1.2 copy-done
  29.2 106.5 %shard_map.64 = f32[9,160,256]{2,1,0:T(8,128)} custom-call(f32[68]{0:T(128)} %multiply_add_fusion.grid_ref, f32[10,160,256]{2,1,0:T(8,128)} %copy-done, f32[96,256]{1,0:T(8,128)} %convert_multiply_fusion.mask_ref, bf16[4,64,96,256]{3,2,1,0:T(8,128)(2,1)} %observed_ref.1, f32[68,4,384]{2,1,0:T(4,128)} %pad.27.taps_ref), custom_call_target="tpu_custom_call" | custom-call | tf_op jit(solution)/shard_map/pallas_call | solution.py:270
  135.6 1.1 constant_dynamic-slice_fusion.3
  136.8 3.2 %collective-permute-start.5 = (f32[9,32,256]{2,1,0:T(8,128)S(1)}, f32[9,32,256]{2,1,0:T(8,128)S(1)}, u32[]{:S(2)}, u32[]{:S(2)}) collective-permute-start(f32[9,32,256]{2,1,0:T(8,128)S(1)} %get-tuple-element.15), channel_id=1, source_target_pairs={{1,0},{2,1},{3,2},{4,3},{5,4},{6,5},{7,6},{9,8},{10,9},{11,10},{12... | collective-permute-start | bytes 884744 | tf_op jit(solution)/shard_map/ppermute | solution.py:20
  140.0 3.1 %collective-permute-start.6 = (f32[9,32,256]{2,1,0:T(8,128)S(1)}, f32[9,32,256]{2,1,0:T(8,128)S(1)}, u32[]{:S(2)}, u32[]{:S(2)}) collective-permute-start(f32[9,32,256]{2,1,0:T(8,128)S(1)} %get-tuple-element.14), channel_id=1, source_target_pairs={{0,1},{1,2},{2,3},{3,4},{4,5},{5,6},{6,7},{8,9},{9,10},{10,11},{11... | collective-permute-start | bytes 884744 | tf_op jit(solution)/shard_map/ppermute | solution.py:20
  143.1 0.0 copy-start.3
  143.1 2.7 %collective-permute-done.5 = f32[9,32,256]{2,1,0:T(8,128)S(1)} collective-permute-done((f32[9,32,256]{2,1,0:T(8,128)S(1)}, f32[9,32,256]{2,1,0:T(8,128)S(1)}, u32[]{:S(2)}, u32[]{:S(2)}) %collective-permute-start.5) | collective-permute-done | bytes 294944 | tf_op jit(solution)/shard_map/ppermute | solution.py:20
  145.9 0.9 collective-permute-done.6
  146.7 1.4 fusion.3
  148.1 0.1 constant_dynamic-slice_fusion.2
  148.2 1.3 collective-permute-start.9
  149.5 0.9 collective-permute-start.8
  150.3 0.6 collective-permute-start.7
  150.9 0.0 copy-done.3
  150.9 1.1 add_reduce_fusion
  152.2 2.7 %collective-permute-done.9 = f32[9,24,256]{2,1,0:T(8,128)S(1)} collective-permute-done((f32[9,24,256]{2,1,0:T(8,128)S(1)}, f32[9,24,256]{2,1,0:T(8,128)S(1)}, u32[]{:S(2)}, u32[]{:S(2)}) %collective-permute-start.9) | collective-permute-done | bytes 221216 | tf_op jit(solution)/shard_map/ppermute | solution.py:25
  154.8 6.4 %collective-permute-done.8 = f32[9,24,256]{2,1,0:T(8,128)S(1)} collective-permute-done((f32[9,24,256]{2,1,0:T(8,128)S(1)}, f32[9,24,256]{2,1,0:T(8,128)S(1)}, u32[]{:S(2)}, u32[]{:S(2)}) %collective-permute-start.8) | collective-permute-done | bytes 221216 | tf_op jit(solution)/shard_map/ppermute | solution.py:25
  161.2 0.0 collective-permute-done.7
  161.2 0.1 add_add_fusion
  161.8 0.0 copy-start.5
  161.8 0.7 copy-done.5
  162.5 0.6 constant_dynamic-update-slice_fusion.1
  (39 shorter events, 0.7 us)
Async XLA Ops:
  0.0 4.5 %copy-start.2 = (bf16[64,4,65]{2,1,0:T(4,128)(2,1)S(1)}, bf16[64,4,65]{2,1,0:T(4,128)(2,1)}, u32[]{:S(2)}) copy-start(bf16[64,4,65]{2,1,0:T(4,128)(2,1)} %param.9) | copy-start | bytes 99844
  0.0 4.6 %copy-start.1 = (bf16[64,4,65]{2,1,0:T(4,128)(2,1)S(1)}, bf16[64,4,65]{2,1,0:T(4,128)(2,1)}, u32[]{:S(2)}) copy-start(bf16[64,4,65]{2,1,0:T(4,128)(2,1)} %param.8) | copy-start | bytes 99844
  1.8 6.4 %collective-permute-start = (f32[9,24,256]{2,1,0:T(8,128)S(1)}, f32[9,24,256]{2,1,0:T(8,128)S(1)}, u32[]{:S(2)}, u32[]{:S(2)}) collective-permute-start(f32[9,24,256]{2,1,0:T(8,128)S(1)} %get-tuple-element.21), channel_id=1, source_target_pairs={{0,8},{8,0},{16,24},{24,16},{1,9},{9,1},{17,25},{25,17},{2,10},{10... | collective-permute-start | bytes 663560 | tf_op jit(solution)/shard_map/ppermute | solution.py:25
  3.0 6.0 %collective-permute-start.1 = (f32[9,24,256]{2,1,0:T(8,128)S(1)}, f32[9,24,256]{2,1,0:T(8,128)S(1)}, u32[]{:S(2)}, u32[]{:S(2)}) collective-permute-start(f32[9,24,256]{2,1,0:T(8,128)S(1)} %get-tuple-element.21), channel_id=1, source_target_pairs={{0,16},{8,24},{16,0},{24,8},{1,17},{9,25},{17,1},{25,9},{2,18},{10... | collective-permute-start | bytes 663560 | tf_op jit(solution)/shard_map/ppermute | solution.py:25
  4.3 9.6 %collective-permute-start.2 = (f32[9,24,256]{2,1,0:T(8,128)S(1)}, f32[9,24,256]{2,1,0:T(8,128)S(1)}, u32[]{:S(2)}, u32[]{:S(2)}) collective-permute-start(f32[9,24,256]{2,1,0:T(8,128)S(1)} %get-tuple-element.21), channel_id=1, source_target_pairs={{0,24},{8,16},{16,8},{24,0},{1,25},{9,17},{17,9},{25,1},{2,26},{10... | collective-permute-start | bytes 663560 | tf_op jit(solution)/shard_map/ppermute | solution.py:25
  6.8 14.2 %copy-start.4 = (s32[96,256]{1,0:T(8,128)S(1)}, s32[96,256]{1,0:T(8,128)}, u32[]{:S(2)}) copy-start(s32[96,256]{1,0:T(8,128)} %param.10) | copy-start | bytes 294916
  14.0 9.6 %collective-permute-start.4 = (f32[9,32,256]{2,1,0:T(8,128)S(1)}, f32[9,32,256]{2,1,0:T(8,128)S(1)}, u32[]{:S(2)}, u32[]{:S(2)}) collective-permute-start(f32[9,32,256]{2,1,0:T(8,128)S(1)} %get-tuple-element.20), channel_id=1, source_target_pairs={{1,0},{2,1},{3,2},{4,3},{5,4},{6,5},{7,6},{9,8},{10,9},{11,10},{12... | collective-permute-start | bytes 884744 | tf_op jit(solution)/shard_map/ppermute | solution.py:20
  17.7 6.8 %collective-permute-start.3 = (f32[9,32,256]{2,1,0:T(8,128)S(1)}, f32[9,32,256]{2,1,0:T(8,128)S(1)}, u32[]{:S(2)}, u32[]{:S(2)}) collective-permute-start(f32[9,32,256]{2,1,0:T(8,128)S(1)} %get-tuple-element.19), channel_id=1, source_target_pairs={{0,1},{1,2},{2,3},{3,4},{4,5},{5,6},{6,7},{8,9},{9,10},{10,11},{11... | collective-permute-start | bytes 884744 | tf_op jit(solution)/shard_map/ppermute | solution.py:20
  28.0 1.2 copy-start
  136.8 9.1 %collective-permute-start.5 = (f32[9,32,256]{2,1,0:T(8,128)S(1)}, f32[9,32,256]{2,1,0:T(8,128)S(1)}, u32[]{:S(2)}, u32[]{:S(2)}) collective-permute-start(f32[9,32,256]{2,1,0:T(8,128)S(1)} %get-tuple-element.15), channel_id=1, source_target_pairs={{1,0},{2,1},{3,2},{4,3},{5,4},{6,5},{7,6},{9,8},{10,9},{11,10},{12... | collective-permute-start | bytes 884744 | tf_op jit(solution)/shard_map/ppermute | solution.py:20
  140.0 6.8 %collective-permute-start.6 = (f32[9,32,256]{2,1,0:T(8,128)S(1)}, f32[9,32,256]{2,1,0:T(8,128)S(1)}, u32[]{:S(2)}, u32[]{:S(2)}) collective-permute-start(f32[9,32,256]{2,1,0:T(8,128)S(1)} %get-tuple-element.14), channel_id=1, source_target_pairs={{0,1},{1,2},{2,3},{3,4},{4,5},{5,6},{6,7},{8,9},{9,10},{10,11},{11... | collective-permute-start | bytes 884744 | tf_op jit(solution)/shard_map/ppermute | solution.py:20
  143.1 7.8 %copy-start.3 = (f32[9,1,6144]{2,1,0:T(1,128)S(1)}, f32[9,1,6144]{2,1,0:T(1,128)}, u32[]{:S(2)}) copy-start(f32[9,1,6144]{2,1,0:T(1,128)} %param.6) | copy-start | bytes 663556
  148.2 6.7 %collective-permute-start.9 = (f32[9,24,256]{2,1,0:T(8,128)S(1)}, f32[9,24,256]{2,1,0:T(8,128)S(1)}, u32[]{:S(2)}, u32[]{:S(2)}) collective-permute-start(f32[9,24,256]{2,1,0:T(8,128)S(1)} %get-tuple-element.17), channel_id=1, source_target_pairs={{0,24},{8,16},{16,8},{24,0},{1,25},{9,17},{17,9},{25,1},{2,26},{10... | collective-permute-start | bytes 663560 | tf_op jit(solution)/shard_map/ppermute | solution.py:25
  149.5 11.8 %collective-permute-start.8 = (f32[9,24,256]{2,1,0:T(8,128)S(1)}, f32[9,24,256]{2,1,0:T(8,128)S(1)}, u32[]{:S(2)}, u32[]{:S(2)}) collective-permute-start(f32[9,24,256]{2,1,0:T(8,128)S(1)} %get-tuple-element.18), channel_id=1, source_target_pairs={{0,16},{8,24},{16,0},{24,8},{1,17},{9,25},{17,1},{25,9},{2,18},{10... | collective-permute-start | bytes 663560 | tf_op jit(solution)/shard_map/ppermute | solution.py:25
  150.3 10.9 %collective-permute-start.7 = (f32[9,24,256]{2,1,0:T(8,128)S(1)}, f32[9,24,256]{2,1,0:T(8,128)S(1)}, u32[]{:S(2)}, u32[]{:S(2)}) collective-permute-start(f32[9,24,256]{2,1,0:T(8,128)S(1)} %get-tuple-element.16), channel_id=1, source_target_pairs={{0,8},{8,0},{16,24},{24,16},{1,9},{9,1},{17,25},{25,17},{2,10},{10... | collective-permute-start | bytes 663560 | tf_op jit(solution)/shard_map/ppermute | solution.py:25
  161.8 0.7 copy-start.5
